TPU v7x, 32 devices: a whole 2x2x4 slice. The times are simulated.
32 devices in a mesh: prow: 8 (over z, x), pcol: 4 (over y, core).
Axes of the slice: x: 2, y: 2, z: 4, core: 2. Of those that a mesh axis runs over, the one named last changes fastest.
Arguments:
- rhs: float32 [31, 64, 2048], P(None, None, 'prow'), may hold values from -6 to 6
- factor: bfloat16 [98, 2048, 2048], P(None, 'prow', 'pcol'), may hold values from -0.03125 to 0.03125
- inverse: bfloat16 [31, 2048, 2048], P(None, 'pcol', 'prow')
- pattern: int32 [98], replicated, may hold values 0 or 1
Outputs:
- solution: float32 [31, 64, 2048], P(None, None, 'prow')
- forward_solution: float32 [31, 64, 2048], P(None, None, 'pcol')
All inputs are finite; a program needn't handle non-finite values.
Results may differ from a plain program's by a relative error of at most 0.011.
Values sent between devices are 32-bit elements; how exact they have to be, the bound alone decides.
A program may use at most 128 MiB of HBM per device.

v0:
```python
import jax
import jax.numpy as jnp
from jax import lax
from jax.sharding import PartitionSpec as P

LEV = 5


def block_start(tree_depth):
    return (tree_depth - 2) * 2**tree_depth + 2


def sum_columns(values):
    result = lax.psum(values, "pcol")
    return lax.optimization_barrier(result)


def sum_rows(values):
    result = lax.psum(values, "prow")
    return lax.optimization_barrier(result)


def per_device(rhs, factor, inverse, pattern):
    live = pattern.astype(jnp.float32)
    partial_value = jnp.zeros(rhs.shape, jnp.float32)
    forward_levels = [None] * LEV
    for tree_depth in range(LEV - 1, -1, -1):
        first = 2**tree_depth - 1
        count = 2**tree_depth
        residual = rhs[first : first + count]
        if tree_depth < LEV - 1:
            residual = residual - sum_columns(partial_value[first : first + count])
        rounded = residual.astype(jnp.bfloat16)
        pieces = jnp.einsum(
            "nrc,nwc->nrw",
            rounded,
            inverse[first : first + count],
            preferred_element_type=jnp.float32,
        )
        forward = sum_rows(pieces)
        forward_levels[tree_depth] = forward
        narrow = forward.astype(jnp.bfloat16)
        if tree_depth > 0:
            start = block_start(tree_depth)
            weights = live[start : start + count * tree_depth].reshape(count, tree_depth)
            for upward in range(1, tree_depth + 1):
                blocks = factor[start + upward - 1 : start + count * tree_depth : tree_depth]
                terms = jnp.einsum(
                    "nrc,nwc->nrw", narrow, blocks, preferred_element_type=jnp.float32
                )
                terms = terms * weights[:, upward - 1][:, None, None]
                groups = count >> upward
                terms = terms.reshape((groups, 2**upward) + terms.shape[1:]).sum(axis=1)
                target = 2 ** (tree_depth - upward) - 1
                partial_value = partial_value.at[target : target + groups].add(terms)
    solved = [None] * LEV
    solved_narrow = [None] * LEV
    for tree_depth in range(LEV):
        first = 2**tree_depth - 1
        count = 2**tree_depth
        target_vec = forward_levels[tree_depth]
        if tree_depth > 0:
            start = block_start(tree_depth)
            weights = live[start : start + count * tree_depth].reshape(count, tree_depth)
            gathered = jnp.zeros(target_vec.shape, jnp.float32)
            for upward in range(1, tree_depth + 1):
                blocks = factor[start + upward - 1 : start + count * tree_depth : tree_depth]
                above = jnp.repeat(solved_narrow[tree_depth - upward], 2**upward, axis=0)
                terms = jnp.einsum(
                    "nrw,nwc->nrc", above, blocks, preferred_element_type=jnp.float32
                )
                gathered = gathered + terms * weights[:, upward - 1][:, None, None]
            target_vec = target_vec - sum_rows(gathered)
        rounded = target_vec.astype(jnp.bfloat16)
        pieces = jnp.einsum(
            "nrw,nwc->nrc",
            rounded,
            inverse[first : first + count],
            preferred_element_type=jnp.float32,
        )
        solution = sum_columns(pieces)
        solved[tree_depth] = solution
        solved_narrow[tree_depth] = solution.astype(jnp.bfloat16)
    return (jnp.concatenate(solved, axis=0), jnp.concatenate(forward_levels, axis=0))


def solution(mesh):
    in_specs = (P(None, None, "prow"), P(None, "prow", "pcol"), P(None, "pcol", "prow"), P())
    out_specs = (P(None, None, "prow"), P(None, None, "pcol"))
    return jax.shard_map(
        per_device, mesh=mesh, in_specs=in_specs, out_specs=out_specs, check_vma=False
    )
```

profile of v0, /device:TPU:0, one launch (start us, length us, event | category | flops | bytes accessed | tf_op | source)
XLA Modules:
  0.0 1112.1 jit_solution(16909229066018414517)
XLA Ops:
  7.2 5.2 fusion.18
  12.9 104.2 %all-reduce.20.cloned.1.call-done = f32[16,64,512]{2,1,0:T(8,128)} async-done(((f32[16,64,512]{2,1,0:T(8,128)}), f32[16,64,512]{2,1,0:T(8,128)}) %all-reduce.20.cloned.1.call-update) | async-done | bytes 2097168 | tf_op jit(solution)/shard_map/psum | solution.py:19
  117.2 1.7 convert_element_type.57
  118.9 3.6 fusion.75
  122.5 3.6 bitcast_reduce_fusion
  126.1 3.6 bitcast_reduce_fusion.1
  129.6 3.6 bitcast_reduce_fusion.2
  133.6 0.8 slice.423
  134.5 33.0 %all-reduce.22.cloned.1.call-done = f32[8,64,256]{2,1,0:T(8,128)} async-done(((f32[8,64,256]{2,1,0:T(8,128)}), f32[8,64,256]{2,1,0:T(8,128)}) %all-reduce.22.cloned.1.call-update) | async-done | bytes 524304 | tf_op jit(solution)/shard_map/psum | solution.py:14
  167.5 3.6 fusion.34
  171.6 78.1 %all-reduce.24.cloned.1.call-done = f32[8,64,512]{2,1,0:T(8,128)} async-done(((f32[8,64,512]{2,1,0:T(8,128)}), f32[8,64,512]{2,1,0:T(8,128)}) %all-reduce.24.cloned.1.call-update) | async-done | bytes 1048592 | tf_op jit(solution)/shard_map/psum | solution.py:19
  249.7 2.7 bitcast_reduce_fusion.3
  252.4 2.7 bitcast_reduce_fusion.4
  255.4 1.3 copy-done.3
  256.6 0.7 slice.426
  257.4 31.7 %all-reduce.26.cloned.1.call-done = f32[4,64,256]{2,1,0:T(8,128)} async-done(((f32[4,64,256]{2,1,0:T(8,128)}), f32[4,64,256]{2,1,0:T(8,128)}) %all-reduce.26.cloned.1.call-update) | async-done | bytes 262160 | tf_op jit(solution)/shard_map/psum | solution.py:14
  289.1 2.6 fusion.90
  292.2 73.2 %all-reduce.28.cloned.1.call-done = f32[4,64,512]{2,1,0:T(8,128)} async-done(((f32[4,64,512]{2,1,0:T(8,128)}), f32[4,64,512]{2,1,0:T(8,128)}) %all-reduce.28.cloned.1.call-update) | async-done | bytes 524304 | tf_op jit(solution)/shard_map/psum | solution.py:19
  365.3 1.8 bitcast_reduce_fusion.5
  367.2 0.7 fusion.127
  367.9 30.9 %all-reduce.30.cloned.1.call-done = f32[2,64,256]{2,1,0:T(8,128)} async-done(((f32[2,64,256]{2,1,0:T(8,128)}), f32[2,64,256]{2,1,0:T(8,128)}) %all-reduce.30.cloned.1.call-update) | async-done | bytes 131088 | tf_op jit(solution)/shard_map/psum | solution.py:14
  398.9 2.2 fusion.102
  401.1 2.4 fusion.78
  403.5 1.7 fusion.81
  405.2 68.2 %all-reduce.32.cloned.1.call-done = f32[2,64,512]{2,1,0:T(8,128)} async-done(((f32[2,64,512]{2,1,0:T(8,128)}), f32[2,64,512]{2,1,0:T(8,128)}) %all-reduce.32.cloned.1.call-update) | async-done | bytes 262160 | tf_op jit(solution)/shard_map/psum | solution.py:19
  473.4 1.4 fusion.82
  474.8 1.5 fusion.122
  476.4 30.5 %all-reduce.34.cloned.1.call-done = f32[1,64,256]{2,1,0:T(8,128)} async-done(((f32[1,64,256]{2,1,0:T(8,128)}), f32[1,64,256]{2,1,0:T(8,128)}) %all-reduce.34.cloned.1.call-update) | async-done | bytes 65552 | tf_op jit(solution)/shard_map/psum | solution.py:14
  506.8 1.9 convolution_bitcast_fusion
  508.8 71.7 %all-reduce.36.cloned.1.call-done = f32[1,64,512]{2,1,0:T(8,128)} async-done(((f32[1,64,512]{2,1,0:T(8,128)}), f32[1,64,512]{2,1,0:T(8,128)}) %all-reduce.36.cloned.1.call-update) | async-done | bytes 131088 | tf_op jit(solution)/shard_map/psum | solution.py:19
  580.5 1.8 convolution_bitcast_fusion.1
  582.4 31.3 %all-reduce.38.cloned.1.call-done = f32[1,64,256]{2,1,0:T(8,128)} async-done(((f32[1,64,256]{2,1,0:T(8,128)}), f32[1,64,256]{2,1,0:T(8,128)}) %all-reduce.38.cloned.1.call-update) | async-done | bytes 65552 | tf_op jit(solution)/shard_map/psum | solution.py:14
  613.7 1.6 convert_bitcast_fusion
  615.3 2.0 convolution_multiply_fusion.2
  617.3 70.9 %all-reduce.40.cloned.1.call-done = f32[2,64,512]{2,1,0:T(8,128)} async-done(((f32[2,64,512]{2,1,0:T(8,128)}), f32[2,64,512]{2,1,0:T(8,128)}) %all-reduce.40.cloned.1.call-update) | async-done | bytes 262160 | tf_op jit(solution)/shard_map/psum | solution.py:19
  688.2 2.1 fusion.100
  690.4 1.5 convolution_multiply_fusion
  691.9 29.9 %all-reduce.42.cloned.1.call-done = f32[2,64,256]{2,1,0:T(8,128)} async-done(((f32[2,64,256]{2,1,0:T(8,128)}), f32[2,64,256]{2,1,0:T(8,128)}) %all-reduce.42.cloned.1.call-update) | async-done | bytes 131088 | tf_op jit(solution)/shard_map/psum | solution.py:14
  721.8 1.6 fusion.137
  723.5 2.3 fusion.65
  725.9 2.1 fusion.62
  727.9 70.3 %all-reduce.44.cloned.1.call-done = f32[4,64,512]{2,1,0:T(8,128)} async-done(((f32[4,64,512]{2,1,0:T(8,128)}), f32[4,64,512]{2,1,0:T(8,128)}) %all-reduce.44.cloned.1.call-update) | async-done | bytes 524304 | tf_op jit(solution)/shard_map/psum | solution.py:19
  798.3 2.4 fusion.88
  800.8 3.0 fusion.59
  803.8 28.3 %all-reduce.46.cloned.1.call-done = f32[4,64,256]{2,1,0:T(8,128)} async-done(((f32[4,64,256]{2,1,0:T(8,128)}), f32[4,64,256]{2,1,0:T(8,128)}) %all-reduce.46.cloned.1.call-update) | async-done | bytes 262160 | tf_op jit(solution)/shard_map/psum | solution.py:14
  832.1 1.8 fusion.136
  833.9 3.4 fusion.56
  837.4 4.4 fusion
  841.8 4.6 fusion.4
  846.4 69.2 %all-reduce.48.cloned.1.call-done = f32[8,64,512]{2,1,0:T(8,128)} async-done(((f32[8,64,512]{2,1,0:T(8,128)}), f32[8,64,512]{2,1,0:T(8,128)}) %all-reduce.48.cloned.1.call-update) | async-done | bytes 1048592 | tf_op jit(solution)/shard_map/psum | solution.py:19
  915.5 3.2 fusion.32
  919.1 4.4 fusion.8
  923.4 28.3 %all-reduce.50.cloned.1.call-done = f32[8,64,256]{2,1,0:T(8,128)} async-done(((f32[8,64,256]{2,1,0:T(8,128)}), f32[8,64,256]{2,1,0:T(8,128)}) %all-reduce.50.cloned.1.call-update) | async-done | bytes 524304 | tf_op jit(solution)/shard_map/psum | solution.py:14
  951.7 2.1 fusion.135
  953.9 6.5 multiply_add_fusion
  960.5 0.7 constant_dynamic-update-slice_fusion.9
  961.2 101.3 %all-reduce.52.cloned.1.call-done = f32[16,64,512]{2,1,0:T(8,128)} async-done(((f32[16,64,512]{2,1,0:T(8,128)}), f32[16,64,512]{2,1,0:T(8,128)}) %all-reduce.52.cloned.1.call-update) | async-done | bytes 2097168 | tf_op jit(solution)/shard_map/psum | solution.py:19
  1062.4 4.6 fusion.16
  1067.0 0.7 constant_dynamic-update-slice_fusion.8
  1067.8 1.9 constant_dynamic-update-slice_fusion.7
  1069.6 1.0 constant_dynamic-update-slice_fusion.6
  1070.7 1.6 constant_dynamic-update-slice_fusion.5
  1072.3 30.7 %all-reduce.54.cloned.1.call-done = f32[16,64,256]{2,1,0:T(8,128)} async-done(((f32[16,64,256]{2,1,0:T(8,128)}), f32[16,64,256]{2,1,0:T(8,128)}) %all-reduce.54.cloned.1.call-update) | async-done | bytes 1048592 | tf_op jit(solution)/shard_map/psum | solution.py:14
  1103.0 2.3 constant_dynamic-update-slice_fusion
  (72 shorter events, 3.0 us)
Async XLA Ops:
  7.2 5.4 copy-start.6
  7.2 110.0 %all-reduce.20.cloned.1.call-start = ((), (), s32[]{:S(2)}) async-start(), calls=%async_computation | async-start | bytes 4194304 | tf_op jit(solution)/shard_map/psum | solution.py:19
  12.5 155.0 %all-reduce.22.cloned.1.call-start = ((), (), s32[]{:S(2)}) async-start(), calls=%async_computation.1 | async-start | bytes 1048576 | tf_op jit(solution)/shard_map/psum | solution.py:14
  134.4 115.3 %all-reduce.24.cloned.1.call-start = ((), (), s32[]{:S(2)}) async-start(), calls=%async_computation.2 | async-start | bytes 2097152 | tf_op jit(solution)/shard_map/psum | solution.py:19
  171.2 118.0 %all-reduce.26.cloned.1.call-start = ((), (), s32[]{:S(2)}) async-start(), calls=%async_computation.3 | async-start | bytes 524288 | tf_op jit(solution)/shard_map/psum | solution.py:14
  255.3 145.8 %copy-start = (f32[8,64,512]{2,1,0:T(8,128)S(1)}, f32[8,64,512]{2,1,0:T(8,128)}, u32[]{:S(2)}) copy-start(f32[8,64,512]{2,1,0:T(8,128)} %all-reduce.24.cloned.1.call-done) | copy-start | bytes 3145732
  255.3 1.3 copy-start.3
  257.4 107.9 %all-reduce.28.cloned.1.call-start = ((), (), s32[]{:S(2)}) async-start(), calls=%async_computation.4 | async-start | bytes 1048576 | tf_op jit(solution)/shard_map/psum | solution.py:19
  291.8 107.1 %all-reduce.30.cloned.1.call-start = ((), (), s32[]{:S(2)}) async-start(), calls=%async_computation.5 | async-start | bytes 262144 | tf_op jit(solution)/shard_map/psum | solution.py:14
  367.8 35.6 %copy-start.2 = (f32[4,64,512]{2,1,0:T(8,128)S(1)}, f32[4,64,512]{2,1,0:T(8,128)}, u32[]{:S(2)}) copy-start(f32[4,64,512]{2,1,0:T(8,128)} %all-reduce.28.cloned.1.call-done) | copy-start | bytes 1572868
  367.9 105.5 %all-reduce.32.cloned.1.call-start = ((), (), s32[]{:S(2)}) async-start(), calls=%async_computation.6 | async-start | bytes 524288 | tf_op jit(solution)/shard_map/psum | solution.py:19
  401.1 105.8 %all-reduce.34.cloned.1.call-start = ((), (), s32[]{:S(2)}) async-start(), calls=%async_computation.7 | async-start | bytes 131072 | tf_op jit(solution)/shard_map/psum | solution.py:14
  476.3 104.2 %all-reduce.36.cloned.1.call-start = ((), (), s32[]{:S(2)}) async-start(), calls=%async_computation.8 | async-start | bytes 262144 | tf_op jit(solution)/shard_map/psum | solution.py:19
  508.8 105.0 %all-reduce.38.cloned.1.call-start = ((), (), s32[]{:S(2)}) async-start(), calls=%async_computation.9 | async-start | bytes 131072 | tf_op jit(solution)/shard_map/psum | solution.py:14
  582.4 105.9 %all-reduce.40.cloned.1.call-start = ((), (), s32[]{:S(2)}) async-start(), calls=%async_computation.10 | async-start | bytes 524288 | tf_op jit(solution)/shard_map/psum | solution.py:19
  617.2 104.6 %all-reduce.42.cloned.1.call-start = ((), (), s32[]{:S(2)}) async-start(), calls=%async_computation.11 | async-start | bytes 262144 | tf_op jit(solution)/shard_map/psum | solution.py:14
  690.3 108.0 %all-reduce.44.cloned.1.call-start = ((), (), s32[]{:S(2)}) async-start(), calls=%async_computation.12 | async-start | bytes 1048576 | tf_op jit(solution)/shard_map/psum | solution.py:19
  725.8 106.3 %all-reduce.46.cloned.1.call-start = ((), (), s32[]{:S(2)}) async-start(), calls=%async_computation.13 | async-start | bytes 524288 | tf_op jit(solution)/shard_map/psum | solution.py:14
  800.7 114.8 %all-reduce.48.cloned.1.call-start = ((), (), s32[]{:S(2)}) async-start(), calls=%async_computation.14 | async-start | bytes 2097152 | tf_op jit(solution)/shard_map/psum | solution.py:19
  837.3 114.4 %all-reduce.50.cloned.1.call-start = ((), (), s32[]{:S(2)}) async-start(), calls=%async_computation.15 | async-start | bytes 1048576 | tf_op jit(solution)/shard_map/psum | solution.py:14
  918.8 143.7 %all-reduce.52.cloned.1.call-start = ((), (), s32[]{:S(2)}) async-start(), calls=%async_computation.16 | async-start | bytes 4194304 | tf_op jit(solution)/shard_map/psum | solution.py:19
  953.9 6.6 copy-start.5
  953.9 108.5 %copy-start.1 = (f32[16,64,512]{2,1,0:T(8,128)S(1)}, f32[16,64,512]{2,1,0:T(8,128)}, u32[]{:S(2)}) copy-start(f32[16,64,512]{2,1,0:T(8,128)} %all-reduce.20.cloned.1.call-done) | copy-start | bytes 6291460
  960.4 142.6 %all-reduce.54.cloned.1.call-start = ((), (), s32[]{:S(2)}) async-start(), calls=%async_computation.17 | async-start | bytes 2097152 | tf_op jit(solution)/shard_map/psum | solution.py:14
  961.2 105.9 %copy-start.4 = (f32[2,64,512]{2,1,0:T(8,128)S(1)}, f32[2,64,512]{2,1,0:T(8,128)}, u32[]{:S(2)}) copy-start(f32[2,64,512]{2,1,0:T(8,128)} %all-reduce.32.cloned.1.call-done) | copy-start | bytes 786436
Sparse Core Ops, SparseCore 0:
  12.6 104.5 all-reduce.19
  134.5 32.8 all-reduce.21
  171.6 78.0 all-reduce.23
  257.5 31.5 all-reduce.25
  292.9 72.3 all-reduce.27
  368.2 30.6 all-reduce.29
  402.8 70.5 all-reduce.31
  476.4 30.3 all-reduce.33
  510.8 69.6 all-reduce.35
  583.3 30.3 all-reduce.37
  617.6 70.5 all-reduce.39
  691.1 30.6 all-reduce.41
  725.9 72.3 all-reduce.43
  800.8 31.2 all-reduce.45
  837.4 78.0 all-reduce.47
  918.9 32.8 all-reduce.49
  960.6 101.8 all-reduce.51
  1067.2 35.7 all-reduce.53
where the time goes:
time: 1110 us
  waiting for transfers between devices  982 us (88%)
  matrix products  90.8 us (8%)
  between operations  14.5 us (1%)
  local copies, waits for them, and re-layouts  12.7 us (1%)
  other arithmetic  11.1 us (1%)
    psum x9, waiting for transfers between devices, sum_rows(): result = lax.psum(values, 'prow')  707 us
    psum x9, waiting for transfers between devices, sum_columns(): result = lax.psum(values, 'pcol')  275 us
    dot_general x10, matrix products, per_device(): jnp.einsum('nrw,nwc->nrc', above, blocks, preferred_element_type=jnp.floa...  34.1 us
    dot_general x10, matrix products, per_device(): jnp.einsum('nrc,nwc->nrw', narrow, blocks, preferred_element_type=jnp.flo...  27 us
  transfers between devices with their start and end apart: 18, of which 18 were waited for; matrix products, arithmetic and copies ran while one was open for 3% of the time, Pallas kernels for 0%

commit v1 on v0

v1 whole, which is shorter than its diff:
```python
import jax
import jax.numpy as jnp
from jax import lax
from jax.experimental import pallas as pl
from jax.experimental.pallas import tpu as pltpu
from jax.sharding import PartitionSpec as P

LEV = 5
CHUNKS = {4: 4, 3: 2, 2: 1, 1: 1, 0: 1}
MESH = pl.DeviceIdType.MESH


def block_start(tree_depth):
    return (tree_depth - 2) * 2**tree_depth + 2


def split_rows(prow):
    minor = 1
    while minor * minor * 4 <= prow:
        minor *= 2
    return prow // minor, minor


def tasks_of(order):
    tasks = []
    for depth in order:
        size = 2**depth // CHUNKS[depth]
        for c in range(CHUNKS[depth]):
            tasks.append((depth, 2**depth - 1 + c * size, size))
    return tasks


def run_tasks(tasks, make, needs):
    done = set()
    live = {}
    waiting = list(tasks)
    while waiting or live:
        for task in list(waiting):
            if all(other in done for other in tasks if needs(task, other)):
                live[task] = make(*task)
                waiting.remove(task)
        for task in list(live):
            try:
                next(live[task])
            except StopIteration:
                done.add(task)
                del live[task]


def overlaps(low_task, high_task):
    depth, first, size = low_task
    up_depth, up_first, up_size = high_task
    if up_depth != depth - 1:
        return False
    parents = {(n + 1) // 2 - 1 for n in range(first, first + size)}
    return any(up_first <= p < up_first + up_size for p in parents)


def make_kernel(A, B, Y, NS, R, WC, WR):
    r = R // (A * B)
    half = R // 2
    inner = 2 ** (LEV - 1) - 1

    def kernel(
        rhs_h, fac_h, inv_h, pat, sol_h, fwd_h,
        rhs, fac, inv, src, recv1, recv2, yout, tout, csrc, cr_f, cr_b, yr_f, yr_b, res, sol,
        lsem, ssem, rsem,
    ):
        prow = lax.axis_index("prow")
        pcol = lax.axis_index("pcol")
        my_a, my_b = prow // B, prow % B
        my_y, my_c = pcol // 2, pcol % 2
        other_c = 1 - my_c
        counter = [0]
        lcounter = [0]

        loads = {}

        def load(key, source, target):
            copy = pltpu.make_async_copy(source, target, lsem.at[lcounter[0]])
            lcounter[0] += 1
            copy.start()
            loads[key] = copy

        def need(key):
            if key in loads:
                loads.pop(key).wait()

        for depth in range(LEV - 1, -1, -1):
            count = 2**depth
            nodes = pl.ds(count - 1, count)
            load(("rhs", depth), rhs_h.at[nodes], rhs.at[nodes])
            load(("inv", depth), inv_h.at[nodes], inv.at[nodes])
            if depth:
                blocks = pl.ds(block_start(depth), count * depth)
                load(("fac", depth), fac_h.at[blocks], fac.at[blocks])

        barrier = pltpu.get_barrier_semaphore()
        peers = [{"prow": my_a * B + (my_b + o) % B} for o in range(1, B)]
        peers += [{"prow": ((my_a + o) % A) * B + my_b} for o in range(1, A)]
        peers += [{"pcol": my_y * 2 + other_c}]
        peers += [{"pcol": ((my_y + o) % Y) * 2 + my_c} for o in range(1, Y)]
        for peer in peers:
            pl.semaphore_signal(barrier, inc=1, device_id=peer, device_id_type=MESH)
        csrc[...] = jnp.zeros(csrc.shape, jnp.float32)
        pl.semaphore_wait(barrier, len(peers))

        def send(source, target, peer):
            k = counter[0]
            counter[0] += 1
            copy = pltpu.make_async_remote_copy(
                src_ref=source, dst_ref=target, send_sem=ssem.at[k], recv_sem=rsem.at[k],
                device_id=peer, device_id_type=MESH,
            )
            copy.start()
            return copy

        def wait_all(copies):
            for copy in copies:
                copy.wait()

        def put_parts(value, n):
            for q in range(A * B):
                src[q // A, q % A, n] = value[q * r : (q + 1) * r]

        def get_parts(ref, n):
            return jnp.concatenate(
                [ref[q // A, q % A, n] for q in range(A * B)], axis=0
            )

        def get_halves(ref, n):
            return jnp.concatenate([ref[0, n], ref[1, n]], axis=0)

        def reduce_rows(first, size, out, finish):
            nodes = pl.ds(first, size)
            copies = []
            for o in range(1, B):
                b = (my_b + o) % B
                copies.append(
                    send(src.at[b, :, nodes], recv1.at[o - 1, :, nodes], {"prow": my_a * B + b})
                )
            yield
            wait_all(copies)
            for o in range(1, B):
                src[my_b, :, nodes] += recv1[o - 1, :, nodes]
            copies = []
            for o in range(1, A):
                a = (my_a + o) % A
                copies.append(
                    send(src.at[my_b, a, nodes], recv2.at[o - 1, nodes], {"prow": a * B + my_b})
                )
            yield
            wait_all(copies)
            total = src[my_b, my_a, nodes]
            for o in range(1, A):
                total = total + recv2[o - 1, nodes]
            out[my_b, my_a, nodes] = finish(total, nodes)
            copies = []
            for o in range(1, A):
                a = (my_a + o) % A
                part = out.at[my_b, my_a, nodes]
                copies.append(send(part, part, {"prow": a * B + my_b}))
            yield
            wait_all(copies)
            copies = []
            for o in range(1, B):
                b = (my_b + o) % B
                part = out.at[my_b, :, nodes]
                copies.append(send(part, part, {"prow": my_a * B + b}))
            yield
            wait_all(copies)

        def reduce_columns(first, size, cr, yr, out, finish):
            nodes = pl.ds(first, size)
            core = {"pcol": my_y * 2 + other_c}
            copies = [send(csrc.at[other_c, nodes], cr.at[nodes], core)]
            yield
            wait_all(copies)
            yr[my_y, nodes] = csrc[my_c, nodes] + cr[nodes]
            copies = []
            for o in range(1, Y):
                part = yr.at[my_y, nodes]
                copies.append(send(part, part, {"pcol": ((my_y + o) % Y) * 2 + my_c}))
            yield
            wait_all(copies)
            total = yr[0, nodes]
            for y in range(1, Y):
                total = total + yr[y, nodes]
            out[my_c, nodes] = finish(total, nodes)
            part = out.at[my_c, nodes]
            copies = [send(part, part, core)]
            yield
            wait_all(copies)

        def forward_task(depth, first, size):
            need(("rhs", depth))
            if depth < LEV - 1:
                mine = pl.ds(pl.multiple_of(my_c * half, half), half)
                yield from reduce_columns(
                    first, size, cr_f, yr_f, res,
                    lambda total, nodes: rhs[nodes, mine] - total,
                )
            need(("inv", depth))

            def solve(n, _):
                value = rhs[n] if depth == LEV - 1 else get_halves(res, n)
                put_parts(
                    lax.dot_general(
                        value.astype(jnp.bfloat16), inv[n], (((1,), (1,)), ((), ())),
                        preferred_element_type=jnp.float32,
                    ),
                    n,
                )
                return _

            lax.fori_loop(first, first + size, solve, 0)
            yield from reduce_rows(first, size, yout, lambda total, nodes: total)
            if depth:
                need(("fac", depth))
                start = block_start(depth)

                def push(m, _):
                    narrow = get_parts(yout, m)
                    base = start + (m - (2**depth - 1)) * depth
                    for up in range(1, depth + 1):
                        weight = pat[base + up - 1].astype(jnp.float32)
                        terms = lax.dot_general(
                            narrow.astype(jnp.bfloat16), fac[base + up - 1],
                            (((1,), (1,)), ((), ())), preferred_element_type=jnp.float32,
                        ) * weight
                        above = (m + 1) // 2**up - 1
                        csrc[0, above] += terms[:half]
                        csrc[1, above] += terms[half:]
                    return _

                lax.fori_loop(first, first + size, push, 0)

        def backward_task(depth, first, size):
            if depth:
                start = block_start(depth)

                def pull(n, _):
                    base = start + (n - (2**depth - 1)) * depth
                    total = jnp.zeros((R, WC), jnp.float32)
                    for up in range(1, depth + 1):
                        above = (n + 1) // 2**up - 1
                        weight = pat[base + up - 1].astype(jnp.float32)
                        total = total + weight * jnp.dot(
                            get_halves(sol, above).astype(jnp.bfloat16), fac[base + up - 1],
                            preferred_element_type=jnp.float32,
                        )
                    put_parts(total, n)
                    return _

                lax.fori_loop(first, first + size, pull, 0)
                yield from reduce_rows(
                    first, size, tout,
                    lambda total, nodes: yout[my_b, my_a, nodes] - total,
                )
            target = tout if depth else yout

            def solve(n, _):
                value = jnp.dot(
                    get_parts(target, n).astype(jnp.bfloat16), inv[n],
                    preferred_element_type=jnp.float32,
                )
                csrc[0, n] = value[:half]
                csrc[1, n] = value[half:]
                return _

            lax.fori_loop(first, first + size, solve, 0)
            yield from reduce_columns(
                first, size, cr_b, yr_b, sol, lambda total, nodes: total
            )

        run_tasks(
            tasks_of(range(LEV - 1, -1, -1)), forward_task, lambda task, other: overlaps(other, task)
        )
        out_copy = pltpu.make_async_copy(yout, fwd_h, lsem.at[lcounter[0]])
        out_copy.start()
        run_tasks(tasks_of(range(LEV)), backward_task, lambda task, other: overlaps(task, other))
        sol_copy = pltpu.make_async_copy(sol, sol_h, lsem.at[lcounter[0] + 1])
        sol_copy.start()
        out_copy.wait()
        sol_copy.wait()

    f32, bf16 = jnp.float32, jnp.bfloat16
    ntask = sum(CHUNKS.values())
    row_sends = 2 * (A - 1 + B - 1)
    col_sends = 1 + Y
    sends = ntask * (row_sends + col_sends) * 2
    blocks = block_start(LEV)
    scratch = [
        pltpu.VMEM((NS, R, WR), f32),
        pltpu.VMEM((blocks, WR, WC), bf16),
        pltpu.VMEM((NS, WC, WR), bf16),
        pltpu.VMEM((B, A, NS, r, WC), f32),
        pltpu.VMEM((B - 1, A, NS, r, WC), f32),
        pltpu.VMEM((A - 1, NS, r, WC), f32),
        pltpu.VMEM((B, A, NS, r, WC), f32),
        pltpu.VMEM((B, A, NS, r, WC), f32),
        pltpu.VMEM((2, NS, half, WR), f32),
        pltpu.VMEM((inner, half, WR), f32),
        pltpu.VMEM((NS, half, WR), f32),
        pltpu.VMEM((Y, inner, half, WR), f32),
        pltpu.VMEM((Y, NS, half, WR), f32),
        pltpu.VMEM((2, inner, half, WR), f32),
        pltpu.VMEM((2, NS, half, WR), f32),
        pltpu.SemaphoreType.DMA((3 * LEV + 2,)),
        pltpu.SemaphoreType.DMA((sends,)),
        pltpu.SemaphoreType.DMA((sends,)),
    ]
    any_spec = pl.BlockSpec(memory_space=pl.ANY)
    return pl.pallas_call(
        kernel,
        out_shape=(
            jax.ShapeDtypeStruct((2, NS, half, WR), f32),
            jax.ShapeDtypeStruct((B, A, NS, r, WC), f32),
        ),
        in_specs=[any_spec, any_spec, any_spec, pl.BlockSpec(memory_space=pltpu.SMEM)],
        out_specs=(any_spec, any_spec),
        scratch_shapes=scratch,
        cost_estimate=pl.CostEstimate(
            flops=4 * R * WR * WC * (blocks + NS),
            bytes_accessed=2 * WR * WC * (blocks + NS) + 8 * NS * R * (WC + WR),
            transcendentals=0,
        ),
        compiler_params=pltpu.CompilerParams(
            collective_id=0, has_side_effects=True, vmem_limit_bytes=64 * 1024 * 1024 - 65536
        ),
    )


def solution(mesh):
    A, B = split_rows(mesh.shape["prow"])
    Y = mesh.shape["pcol"] // 2

    def per_device(rhs, factor, inverse, pattern):
        NS, R, WR = rhs.shape
        WC = inverse.shape[1]
        sol, fwd = make_kernel(A, B, Y, NS, R, WC, WR)(rhs, factor, inverse, pattern)
        sol = jnp.transpose(sol, (1, 0, 2, 3)).reshape(NS, R, WR)
        fwd = jnp.transpose(fwd, (2, 0, 1, 3, 4)).reshape(NS, R, WC)
        return sol, fwd

    in_specs = (P(None, None, "prow"), P(None, "prow", "pcol"), P(None, "pcol", "prow"), P())
    out_specs = (P(None, None, "prow"), P(None, None, "pcol"))
    return jax.shard_map(
        per_device, mesh=mesh, in_specs=in_specs, out_specs=out_specs, check_vma=False
    )
```

time: 1110 us -> 411 us (0.37)
  waiting for transfers between devices: 982 us -> 0 us
  Pallas kernels: 0 us -> 401 us
  matrix products: 90.8 us -> 0 us
  between operations: 14.5 us -> 0.65 us
  other arithmetic: 11.1 us -> 0 us
    psum x18 -> x0, waiting for transfers between devices: 982 us -> none  [the longest x9 707 us: sum_rows(): result = lax.psum(values, 'prow')]
    pallas_call x0 -> x1, Pallas kernels: none -> 401 us  [per_device(): make_kernel(A, B, Y, NS, R, WC, WR)(rhs, factor, inverse, pattern)]
    dot_general x30 -> x0, matrix products: 90.8 us -> none  [the longest x10 34.1 us: per_device(): jnp.einsum('nrw,nwc->nrc', above, blocks, preferred_element_type=jnp.floa...]
  transfers between devices with their start and end apart: 18 -> 0, of which waited for: 18 -> 0; matrix products, arithmetic and copies ran while one was open for 3% -> 0% of each run, Pallas kernels for 0% -> 0%
where the time goes in v1:
time: 411 us; the launch traced here: 407 us
  Pallas kernels  401 us (98%)
  local copies, waits for them, and re-layouts  5.84 us (1%)
    pallas_call x1, Pallas kernels, per_device(): make_kernel(A, B, Y, NS, R, WC, WR)(rhs, factor, inverse, pattern)  401 us

profile of v1, /device:TPU:0, one launch (start us, length us, event | category | flops | bytes accessed | tf_op | source)
XLA Modules:
  0.0 407.4 jit_solution(7940432201783481904)
XLA Ops:
  0.6 400.9 %shard_map.59 = (f32[2,31,32,256]{3,2,1,0:T(8,128)}, f32[2,4,31,8,512]{4,3,2,1,0:T(8,128)}) custom-call(f32[31,64,256]{2,1,0:T(8,128)} %rhs_h.1, bf16[98,256,512]{2,1,0:T(8,128)(2,1)} %fac_h.1, bf16[31,512,256]{2,1,0:T(8,128)(2,1)} %inv_h.1, s32[98]{0:T(128)} %pat.1), custom_call_target="tpu_custom_call" | custom-call | flops 4328521728 | bytes 46006272 | tf_op jit(solution)/shard_map/pallas_call | solution.py:341
  401.5 0.0 copy-start
  401.5 3.3 copy.6
  404.8 0.0 copy-done
  404.8 2.6 copy.7
Async XLA Ops:
  401.5 3.3 copy-start

commit v2 on v1

--- a/solution.py
+++ b/solution.py
@@ -1,3 +1,5 @@
+import functools
+
 import jax
 import jax.numpy as jnp
 from jax import lax
@@ -6,7 +8,8 @@
 from jax.sharding import PartitionSpec as P
 
 LEV = 5
-CHUNKS = {4: 4, 3: 2, 2: 1, 1: 1, 0: 1}
+CHUNKS = {4: 8, 3: 4, 2: 2, 1: 1, 0: 1}
+DIRECT = 2
 MESH = pl.DeviceIdType.MESH
 
 
@@ -30,21 +33,41 @@
     return tasks
 
 
-def run_tasks(tasks, make, needs):
+def run_tasks(tasks, make, needs, fillers, filler_needs, blocks):
     done = set()
     live = {}
+    heavy = []
     waiting = list(tasks)
-    while waiting or live:
+    left = list(fillers)
+
+    def advance(task):
+        try:
+            if next(live[task]) == "matmul":
+                heavy.append(task)
+        except StopIteration:
+            done.add(task)
+            del live[task]
+
+    while waiting or live or left:
+        started = set()
         for task in list(waiting):
-            if all(other in done for other in tasks if needs(task, other)):
+            ready = all(other in done for other in tasks if needs(task, other))
+            ready = ready and not any(blocks(filler, task) for filler in left)
+            if ready and task[0] not in started:
+                started.add(task[0])
                 live[task] = make(*task)
                 waiting.remove(task)
         for task in list(live):
-            try:
-                next(live[task])
-            except StopIteration:
-                done.add(task)
-                del live[task]
+            if task not in heavy:
+                advance(task)
+        for task in list(heavy):
+            heavy.remove(task)
+            advance(task)
+        for filler in list(left):
+            if all(other in done for other in tasks if filler_needs(filler, other)):
+                left.remove(filler)
+                fillers[filler]()
+                break
 
 
 def overlaps(low_task, high_task):
@@ -56,6 +79,15 @@
     return any(up_first <= p < up_first + up_size for p in parents)
 
 
+def far_above(low_task, high_task):
+    depth, first, size = low_task
+    up_depth, up_first, up_size = high_task
+    if up_depth > depth - 2:
+        return False
+    above = {(n + 1) // 2 ** (depth - up_depth) - 1 for n in range(first, first + size)}
+    return any(up_first <= p < up_first + up_size for p in above)
+
+
 def make_kernel(A, B, Y, NS, R, WC, WR):
     r = R // (A * B)
     half = R // 2
@@ -63,7 +95,7 @@
 
     def kernel(
         rhs_h, fac_h, inv_h, pat, sol_h, fwd_h,
-        rhs, fac, inv, src, recv1, recv2, yout, tout, csrc, cr_f, cr_b, yr_f, yr_b, res, sol,
+        rhs, fac, inv, src, recv1, recv2, recv3, yout, tout, csrc, cr_f, cr_b, yr_f, yr_b, res, sol,
         lsem, ssem, rsem,
     ):
         prow = lax.axis_index("prow")
@@ -96,8 +128,7 @@
                 load(("fac", depth), fac_h.at[blocks], fac.at[blocks])
 
         barrier = pltpu.get_barrier_semaphore()
-        peers = [{"prow": my_a * B + (my_b + o) % B} for o in range(1, B)]
-        peers += [{"prow": ((my_a + o) % A) * B + my_b} for o in range(1, A)]
+        peers = [{"prow": (prow + o) % (A * B)} for o in range(1, A * B)]
         peers += [{"pcol": my_y * 2 + other_c}]
         peers += [{"pcol": ((my_y + o) % Y) * 2 + my_c} for o in range(1, Y)]
         for peer in peers:
@@ -121,17 +152,39 @@
 
         def put_parts(value, n):
             for q in range(A * B):
-                src[q // A, q % A, n] = value[q * r : (q + 1) * r]
+                src[q % B, q // B, n] = value[q * r : (q + 1) * r]
 
         def get_parts(ref, n):
             return jnp.concatenate(
-                [ref[q // A, q % A, n] for q in range(A * B)], axis=0
+                [ref[q % B, q // B, n] for q in range(A * B)], axis=0
             )
 
         def get_halves(ref, n):
             return jnp.concatenate([ref[0, n], ref[1, n]], axis=0)
 
-        def reduce_rows(first, size, out, finish):
+        def reduce_rows_direct(first, size, out, finish):
+            nodes = pl.ds(first, size)
+            others = [(prow + o) % (A * B) for o in range(1, A * B)]
+            copies = []
+            for k, q in enumerate(others):
+                copies.append(
+                    send(src.at[q % B, q // B, nodes], recv3.at[k, nodes], {"prow": q})
+                )
+            yield
+            wait_all(copies)
+            total = src[my_b, my_a, nodes]
+            for k in range(A * B - 1):
+                total = total + recv3[k, nodes]
+            out[my_b, my_a, nodes] = finish(total, nodes)
+            part = out.at[my_b, my_a, nodes]
+            copies = [send(part, part, {"prow": q}) for q in others]
+            yield
+            wait_all(copies)
+
+        def reduce_rows(depth, first, size, out, finish):
+            if depth <= DIRECT:
+                yield from reduce_rows_direct(first, size, out, finish)
+                return
             nodes = pl.ds(first, size)
             copies = []
             for o in range(1, B):
@@ -170,7 +223,7 @@
             yield
             wait_all(copies)
 
-        def reduce_columns(first, size, cr, yr, out, finish):
+        def reduce_columns(depth, first, size, cr, yr, out, finish):
             nodes = pl.ds(first, size)
             core = {"pcol": my_y * 2 + other_c}
             copies = [send(csrc.at[other_c, nodes], cr.at[nodes], core)]
@@ -197,9 +250,10 @@
             if depth < LEV - 1:
                 mine = pl.ds(pl.multiple_of(my_c * half, half), half)
                 yield from reduce_columns(
-                    first, size, cr_f, yr_f, res,
+                    depth, first, size, cr_f, yr_f, res,
                     lambda total, nodes: rhs[nodes, mine] - total,
                 )
+                yield "matmul"
             need(("inv", depth))
 
             def solve(n, _):
@@ -214,49 +268,57 @@
                 return _
 
             lax.fori_loop(first, first + size, solve, 0)
-            yield from reduce_rows(first, size, yout, lambda total, nodes: total)
+            yield from reduce_rows(depth, first, size, yout, lambda total, nodes: total)
             if depth:
-                need(("fac", depth))
-                start = block_start(depth)
-
-                def push(m, _):
-                    narrow = get_parts(yout, m)
-                    base = start + (m - (2**depth - 1)) * depth
-                    for up in range(1, depth + 1):
-                        weight = pat[base + up - 1].astype(jnp.float32)
-                        terms = lax.dot_general(
-                            narrow.astype(jnp.bfloat16), fac[base + up - 1],
-                            (((1,), (1,)), ((), ())), preferred_element_type=jnp.float32,
-                        ) * weight
-                        above = (m + 1) // 2**up - 1
-                        csrc[0, above] += terms[:half]
-                        csrc[1, above] += terms[half:]
-                    return _
-
-                lax.fori_loop(first, first + size, push, 0)
+                yield "matmul"
+                push_up(depth, first, size, [1])
+
+        def push_up(depth, first, size, ups):
+            need(("fac", depth))
+            start = block_start(depth)
+
+            def push(m, _):
+                narrow = get_parts(yout, m)
+                base = start + (m - (2**depth - 1)) * depth
+                for up in ups:
+                    weight = pat[base + up - 1].astype(jnp.float32)
+                    terms = lax.dot_general(
+                        narrow.astype(jnp.bfloat16), fac[base + up - 1],
+                        (((1,), (1,)), ((), ())), preferred_element_type=jnp.float32,
+                    ) * weight
+                    above = (m + 1) // 2**up - 1
+                    csrc[0, above] += terms[:half]
+                    csrc[1, above] += terms[half:]
+                return _
+
+            lax.fori_loop(first, first + size, push, 0)
+
+        def pull_down(depth, first, size, ups, add):
+            start = block_start(depth)
+
+            def pull(n, _):
+                base = start + (n - (2**depth - 1)) * depth
+                total = get_parts(src, n) if add else jnp.zeros((R, WC), jnp.float32)
+                for up in ups:
+                    above = (n + 1) // 2**up - 1
+                    weight = pat[base + up - 1].astype(jnp.float32)
+                    total = total + weight * jnp.dot(
+                        get_halves(sol, above).astype(jnp.bfloat16), fac[base + up - 1],
+                        preferred_element_type=jnp.float32,
+                    )
+                put_parts(total, n)
+                return _
+
+            lax.fori_loop(first, first + size, pull, 0)
 
         def backward_task(depth, first, size):
             if depth:
-                start = block_start(depth)
-
-                def pull(n, _):
-                    base = start + (n - (2**depth - 1)) * depth
-                    total = jnp.zeros((R, WC), jnp.float32)
-                    for up in range(1, depth + 1):
-                        above = (n + 1) // 2**up - 1
-                        weight = pat[base + up - 1].astype(jnp.float32)
-                        total = total + weight * jnp.dot(
-                            get_halves(sol, above).astype(jnp.bfloat16), fac[base + up - 1],
-                            preferred_element_type=jnp.float32,
-                        )
-                    put_parts(total, n)
-                    return _
-
-                lax.fori_loop(first, first + size, pull, 0)
+                pull_down(depth, first, size, [1], depth > 1)
                 yield from reduce_rows(
-                    first, size, tout,
+                    depth, first, size, tout,
                     lambda total, nodes: yout[my_b, my_a, nodes] - total,
                 )
+                yield "matmul"
             target = tout if depth else yout
 
             def solve(n, _):
@@ -270,25 +332,38 @@
 
             lax.fori_loop(first, first + size, solve, 0)
             yield from reduce_columns(
-                first, size, cr_b, yr_b, sol, lambda total, nodes: total
+                depth, first, size, cr_b, yr_b, sol, lambda total, nodes: total
             )
 
+        up_tasks = tasks_of(range(LEV - 1, -1, -1))
+        late = {
+            t: functools.partial(push_up, *t, range(2, t[0] + 1)) for t in up_tasks if t[0] > 1
+        }
         run_tasks(
-            tasks_of(range(LEV - 1, -1, -1)), forward_task, lambda task, other: overlaps(other, task)
+            up_tasks, forward_task, lambda task, other: overlaps(other, task),
+            late, lambda filler, other: other == filler, far_above,
         )
         out_copy = pltpu.make_async_copy(yout, fwd_h, lsem.at[lcounter[0]])
         out_copy.start()
-        run_tasks(tasks_of(range(LEV)), backward_task, lambda task, other: overlaps(task, other))
+        down_tasks = tasks_of(range(LEV))
+        early = {
+            t: functools.partial(pull_down, *t, range(2, t[0] + 1), False)
+            for t in down_tasks if t[0] > 1
+        }
+        run_tasks(
+            down_tasks, backward_task, overlaps,
+            early, far_above, lambda filler, task: filler == task,
+        )
         sol_copy = pltpu.make_async_copy(sol, sol_h, lsem.at[lcounter[0] + 1])
         sol_copy.start()
         out_copy.wait()
         sol_copy.wait()
 
     f32, bf16 = jnp.float32, jnp.bfloat16
-    ntask = sum(CHUNKS.values())
-    row_sends = 2 * (A - 1 + B - 1)
-    col_sends = 1 + Y
-    sends = ntask * (row_sends + col_sends) * 2
+    sends = 0
+    for depth in range(LEV):
+        rows = A * B - 1 if depth <= DIRECT else A + B - 2
+        sends += CHUNKS[depth] * 2 * (2 * rows + 1 + Y)
     blocks = block_start(LEV)
     scratch = [
         pltpu.VMEM((NS, R, WR), f32),
@@ -297,6 +372,7 @@
         pltpu.VMEM((B, A, NS, r, WC), f32),
         pltpu.VMEM((B - 1, A, NS, r, WC), f32),
         pltpu.VMEM((A - 1, NS, r, WC), f32),
+        pltpu.VMEM((A * B - 1, 2 ** (DIRECT + 1) - 1, r, WC), f32),
         pltpu.VMEM((B, A, NS, r, WC), f32),
         pltpu.VMEM((B, A, NS, r, WC), f32),
         pltpu.VMEM((2, NS, half, WR), f32),
@@ -340,7 +416,7 @@
         WC = inverse.shape[1]
         sol, fwd = make_kernel(A, B, Y, NS, R, WC, WR)(rhs, factor, inverse, pattern)
         sol = jnp.transpose(sol, (1, 0, 2, 3)).reshape(NS, R, WR)
-        fwd = jnp.transpose(fwd, (2, 0, 1, 3, 4)).reshape(NS, R, WC)
+        fwd = jnp.transpose(fwd, (2, 1, 0, 3, 4)).reshape(NS, R, WC)
         return sol, fwd
 
     in_specs = (P(None, None, "prow"), P(None, "prow", "pcol"), P(None, "pcol", "prow"), P())

time: 411 us -> 372 us (0.905)
  Pallas kernels: 401 us -> 366 us
    pallas_call x1, Pallas kernels: 401 us -> 366 us  [per_device(): make_kernel(A, B, Y, NS, R, WC, WR)(rhs, factor, inverse, pattern)]
where the time goes in v2:
time: 372 us
  Pallas kernels  366 us (98%)
  local copies, waits for them, and re-layouts  5.84 us (2%)
    pallas_call x1, Pallas kernels, per_device(): make_kernel(A, B, Y, NS, R, WC, WR)(rhs, factor, inverse, pattern)  366 us

profile of v2, /device:TPU:0, one launch (start us, length us, event | category | flops | bytes accessed | tf_op | source)
XLA Modules:
  0.0 372.1 jit_solution(16693630582349414780)
XLA Ops:
  0.6 365.6 %shard_map.59 = (f32[2,31,32,256]{3,2,1,0:T(8,128)}, f32[2,4,31,8,512]{4,3,2,1,0:T(8,128)}) custom-call(f32[31,64,256]{2,1,0:T(8,128)} %rhs_h.1, bf16[98,256,512]{2,1,0:T(8,128)(2,1)} %fac_h.1, bf16[31,512,256]{2,1,0:T(8,128)(2,1)} %inv_h.1, s32[98]{0:T(128)} %pat.1), custom_call_target="tpu_custom_call" | custom-call | flops 4328521728 | bytes 46006272 | tf_op jit(solution)/shard_map/pallas_call | solution.py:417
  366.2 0.0 copy-start
  366.2 3.3 copy.6
  369.5 0.0 copy-done
  369.5 2.6 copy.7
Async XLA Ops:
  366.2 3.3 copy-start

commit v3 on v2

--- a/solution.py
+++ b/solution.py
@@ -8,7 +8,7 @@
 from jax.sharding import PartitionSpec as P
 
 LEV = 5
-CHUNKS = {4: 8, 3: 4, 2: 2, 1: 1, 0: 1}
+CHUNKS = {4: 8, 3: 8, 2: 4, 1: 2, 0: 1}
 DIRECT = 2
 MESH = pl.DeviceIdType.MESH
 
@@ -79,6 +79,13 @@
     return any(up_first <= p < up_first + up_size for p in parents)
 
 
+def few_in_flight(depth, first, forward):
+    if depth == DIRECT + 1:
+        place = first - (2**depth - 1)
+        return place >= 2**depth * 3 // 4 if forward else place < 2**depth // 4
+    return depth <= DIRECT
+
+
 def far_above(low_task, high_task):
     depth, first, size = low_task
     up_depth, up_first, up_size = high_task
@@ -95,7 +102,7 @@
 
     def kernel(
         rhs_h, fac_h, inv_h, pat, sol_h, fwd_h,
-        rhs, fac, inv, src, recv1, recv2, recv3, yout, tout, csrc, cr_f, cr_b, yr_f, yr_b, res, sol,
+        rhs, fac, inv, src, recv1, recv2, recv3, recv4, yout, tout, csrc, cr_f, cr_b, yr_f, yr_b, sol,
         lsem, ssem, rsem,
     ):
         prow = lax.axis_index("prow")
@@ -129,8 +136,7 @@
 
         barrier = pltpu.get_barrier_semaphore()
         peers = [{"prow": (prow + o) % (A * B)} for o in range(1, A * B)]
-        peers += [{"pcol": my_y * 2 + other_c}]
-        peers += [{"pcol": ((my_y + o) % Y) * 2 + my_c} for o in range(1, Y)]
+        peers += [{"pcol": (pcol + o) % (2 * Y)} for o in range(1, 2 * Y)]
         for peer in peers:
             pl.semaphore_signal(barrier, inc=1, device_id=peer, device_id_type=MESH)
         csrc[...] = jnp.zeros(csrc.shape, jnp.float32)
@@ -182,7 +188,7 @@
             wait_all(copies)
 
         def reduce_rows(depth, first, size, out, finish):
-            if depth <= DIRECT:
+            if few_in_flight(depth, first, out is yout):
                 yield from reduce_rows_direct(first, size, out, finish)
                 return
             nodes = pl.ds(first, size)
@@ -223,7 +229,27 @@
             yield
             wait_all(copies)
 
+        def reduce_columns_direct(first, size, slot, finish):
+            nodes, slots = pl.ds(first, size), pl.ds(slot, size)
+            recv4[pcol, slots] = jnp.stack([csrc[0, nodes], csrc[1, nodes]], axis=1)
+            copies = []
+            for o in range(1, 2 * Y):
+                part = recv4.at[pcol, slots]
+                copies.append(send(part, part, {"pcol": (pcol + o) % (2 * Y)}))
+            yield
+            wait_all(copies)
+            for c in range(2):
+                total = recv4[0, slots, c]
+                for q in range(1, 2 * Y):
+                    total = total + recv4[q, slots, c]
+                sol[c, nodes] = finish(total, nodes, pl.ds(c * half, half))
+
         def reduce_columns(depth, first, size, cr, yr, out, finish):
+            if depth <= DIRECT:
+                slot = 2 ** (DIRECT + 1) - 1 if cr is cr_b and depth == 0 else first
+                yield from reduce_columns_direct(first, size, slot, finish)
+                return
+            mine = pl.ds(pl.multiple_of(my_c * half, half), half)
             nodes = pl.ds(first, size)
             core = {"pcol": my_y * 2 + other_c}
             copies = [send(csrc.at[other_c, nodes], cr.at[nodes], core)]
@@ -239,7 +265,7 @@
             total = yr[0, nodes]
             for y in range(1, Y):
                 total = total + yr[y, nodes]
-            out[my_c, nodes] = finish(total, nodes)
+            out[my_c, nodes] = finish(total, nodes, mine)
             part = out.at[my_c, nodes]
             copies = [send(part, part, core)]
             yield
@@ -248,16 +274,15 @@
         def forward_task(depth, first, size):
             need(("rhs", depth))
             if depth < LEV - 1:
-                mine = pl.ds(pl.multiple_of(my_c * half, half), half)
                 yield from reduce_columns(
-                    depth, first, size, cr_f, yr_f, res,
-                    lambda total, nodes: rhs[nodes, mine] - total,
+                    depth, first, size, cr_f, yr_f, sol,
+                    lambda total, nodes, mine: rhs[nodes, mine] - total,
                 )
                 yield "matmul"
             need(("inv", depth))
 
             def solve(n, _):
-                value = rhs[n] if depth == LEV - 1 else get_halves(res, n)
+                value = rhs[n] if depth == LEV - 1 else get_halves(sol, n)
                 put_parts(
                     lax.dot_general(
                         value.astype(jnp.bfloat16), inv[n], (((1,), (1,)), ((), ())),
@@ -267,7 +292,7 @@
                 )
                 return _
 
-            lax.fori_loop(first, first + size, solve, 0)
+            lax.fori_loop(first, first + size, solve, 0, unroll=True)
             yield from reduce_rows(depth, first, size, yout, lambda total, nodes: total)
             if depth:
                 yield "matmul"
@@ -291,7 +316,7 @@
                     csrc[1, above] += terms[half:]
                 return _
 
-            lax.fori_loop(first, first + size, push, 0)
+            lax.fori_loop(first, first + size, push, 0, unroll=True)
 
         def pull_down(depth, first, size, ups, add):
             start = block_start(depth)
@@ -309,7 +334,7 @@
                 put_parts(total, n)
                 return _
 
-            lax.fori_loop(first, first + size, pull, 0)
+            lax.fori_loop(first, first + size, pull, 0, unroll=True)
 
         def backward_task(depth, first, size):
             if depth:
@@ -330,9 +355,9 @@
                 csrc[1, n] = value[half:]
                 return _
 
-            lax.fori_loop(first, first + size, solve, 0)
+            lax.fori_loop(first, first + size, solve, 0, unroll=True)
             yield from reduce_columns(
-                depth, first, size, cr_b, yr_b, sol, lambda total, nodes: total
+                depth, first, size, cr_b, yr_b, sol, lambda total, nodes, mine: total
             )
 
         up_tasks = tasks_of(range(LEV - 1, -1, -1))
@@ -362,8 +387,9 @@
     f32, bf16 = jnp.float32, jnp.bfloat16
     sends = 0
     for depth in range(LEV):
-        rows = A * B - 1 if depth <= DIRECT else A + B - 2
-        sends += CHUNKS[depth] * 2 * (2 * rows + 1 + Y)
+        rows = A * B - 1 if depth <= DIRECT + 1 else A + B - 2
+        cols = 2 * Y - 1 if depth <= DIRECT else 1 + Y
+        sends += CHUNKS[depth] * 2 * (2 * rows + cols)
     blocks = block_start(LEV)
     scratch = [
         pltpu.VMEM((NS, R, WR), f32),
@@ -372,7 +398,8 @@
         pltpu.VMEM((B, A, NS, r, WC), f32),
         pltpu.VMEM((B - 1, A, NS, r, WC), f32),
         pltpu.VMEM((A - 1, NS, r, WC), f32),
-        pltpu.VMEM((A * B - 1, 2 ** (DIRECT + 1) - 1, r, WC), f32),
+        pltpu.VMEM((A * B - 1, 2 ** (DIRECT + 2) - 1, r, WC), f32),
+        pltpu.VMEM((2 * Y, 2 ** (DIRECT + 1), 2, half, WR), f32),
         pltpu.VMEM((B, A, NS, r, WC), f32),
         pltpu.VMEM((B, A, NS, r, WC), f32),
         pltpu.VMEM((2, NS, half, WR), f32),
@@ -380,7 +407,6 @@
         pltpu.VMEM((NS, half, WR), f32),
         pltpu.VMEM((Y, inner, half, WR), f32),
         pltpu.VMEM((Y, NS, half, WR), f32),
-        pltpu.VMEM((2, inner, half, WR), f32),
         pltpu.VMEM((2, NS, half, WR), f32),
         pltpu.SemaphoreType.DMA((3 * LEV + 2,)),
         pltpu.SemaphoreType.DMA((sends,)),

time: 372 us -> 362 us (0.973)
  Pallas kernels: 366 us -> 356 us
    pallas_call x1, Pallas kernels: 366 us -> 356 us  [per_device(): make_kernel(A, B, Y, NS, R, WC, WR)(rhs, factor, inverse, pattern)]
where the time goes in v3:
time: 362 us
  Pallas kernels  356 us (98%)
  local copies, waits for them, and re-layouts  5.84 us (2%)
    pallas_call x1, Pallas kernels, per_device(): make_kernel(A, B, Y, NS, R, WC, WR)(rhs, factor, inverse, pattern)  356 us

profile of v3, /device:TPU:0, one launch (start us, length us, event | category | flops | bytes accessed | tf_op | source)
XLA Modules:
  0.0 362.2 jit_solution(14429797928445571925)
XLA Ops:
  0.6 355.7 %shard_map.59 = (f32[2,31,32,256]{3,2,1,0:T(8,128)}, f32[2,4,31,8,512]{4,3,2,1,0:T(8,128)}) custom-call(f32[31,64,256]{2,1,0:T(8,128)} %rhs_h.1, bf16[98,256,512]{2,1,0:T(8,128)(2,1)} %fac_h.1, bf16[31,512,256]{2,1,0:T(8,128)(2,1)} %inv_h.1, s32[98]{0:T(128)} %pat.1), custom_call_target="tpu_custom_call" | custom-call | flops 4328521728 | bytes 46006272 | tf_op jit(solution)/shard_map/pallas_call | solution.py:443
  356.4 0.0 copy-start
  356.4 3.3 copy.6
  359.6 0.0 copy-done
  359.6 2.6 copy.7
Async XLA Ops:
  356.4 3.3 copy-start

commit v4 on v3

--- a/solution.py
+++ b/solution.py
@@ -8,7 +8,7 @@
 from jax.sharding import PartitionSpec as P
 
 LEV = 5
-CHUNKS = {4: 8, 3: 8, 2: 4, 1: 2, 0: 1}
+CHUNKS = {4: 4, 3: 4, 2: 2, 1: 1, 0: 1}
 DIRECT = 2
 MESH = pl.DeviceIdType.MESH
 
@@ -292,7 +292,7 @@
                 )
                 return _
 
-            lax.fori_loop(first, first + size, solve, 0, unroll=True)
+            lax.fori_loop(first, first + size, solve, 0)
             yield from reduce_rows(depth, first, size, yout, lambda total, nodes: total)
             if depth:
                 yield "matmul"
@@ -316,7 +316,7 @@
                     csrc[1, above] += terms[half:]
                 return _
 
-            lax.fori_loop(first, first + size, push, 0, unroll=True)
+            lax.fori_loop(first, first + size, push, 0)
 
         def pull_down(depth, first, size, ups, add):
             start = block_start(depth)
@@ -334,7 +334,7 @@
                 put_parts(total, n)
                 return _
 
-            lax.fori_loop(first, first + size, pull, 0, unroll=True)
+            lax.fori_loop(first, first + size, pull, 0)
 
         def backward_task(depth, first, size):
             if depth:
@@ -355,7 +355,7 @@
                 csrc[1, n] = value[half:]
                 return _
 
-            lax.fori_loop(first, first + size, solve, 0, unroll=True)
+            lax.fori_loop(first, first + size, solve, 0)
             yield from reduce_columns(
                 depth, first, size, cr_b, yr_b, sol, lambda total, nodes, mine: total
             )

time: 362 us -> 378 us (1.044)
  Pallas kernels: 356 us -> 371 us
    pallas_call x1, Pallas kernels: 356 us -> 371 us  [per_device(): make_kernel(A, B, Y, NS, R, WC, WR)(rhs, factor, inverse, pattern)]
where the time goes in v4:
time: 378 us
  Pallas kernels  371 us (98%)
  local copies, waits for them, and re-layouts  5.84 us (2%)
    pallas_call x1, Pallas kernels, per_device(): make_kernel(A, B, Y, NS, R, WC, WR)(rhs, factor, inverse, pattern)  371 us

profile of v4, /device:TPU:0, one launch (start us, length us, event | category | flops | bytes accessed | tf_op | source)
XLA Modules:
  0.0 377.6 jit_solution(10323483540118763697)
XLA Ops:
  0.6 371.1 %shard_map.59 = (f32[2,31,32,256]{3,2,1,0:T(8,128)}, f32[2,4,31,8,512]{4,3,2,1,0:T(8,128)}) custom-call(f32[31,64,256]{2,1,0:T(8,128)} %rhs_h.1, bf16[98,256,512]{2,1,0:T(8,128)(2,1)} %fac_h.1, bf16[31,512,256]{2,1,0:T(8,128)(2,1)} %inv_h.1, s32[98]{0:T(128)} %pat.1), custom_call_target="tpu_custom_call" | custom-call | flops 4328521728 | bytes 46006272 | tf_op jit(solution)/shard_map/pallas_call | solution.py:443
  371.7 0.0 copy-start
  371.8 3.3 copy.6
  375.0 0.0 copy-done
  375.0 2.6 copy.7
Async XLA Ops:
  371.7 3.3 copy-start
